TPU v7x, 256 devices: a whole 4x4x8 slice. The times are simulated.
256 devices in a mesh: expert: 128 (over y, x, z), shard: 2 (over core).
Axes of the slice: x: 4, y: 4, z: 8, core: 2. Of those that a mesh axis runs over, the one named last changes fastest.
Arguments:
- tokens: bfloat16 [32768, 2048], P(('expert', 'shard')), may hold values from -6 to 6
- router: bfloat16 [2048, 64], replicated, may hold values from -0.125 to 0.125
- w_gate: bfloat16 [128, 2048, 704], P('expert', None, 'shard'), may hold values from -0.125 to 0.125
- w_up: bfloat16 [128, 2048, 704], P('expert', None, 'shard'), may hold values from -0.125 to 0.125
- w_down: bfloat16 [128, 704, 2048], P('expert', 'shard'), may hold values from -0.15625 to 0.15625
- picks: int32 [256, 64, 8], P(('expert', 'shard')), may hold values from 0 to 127, as said below
- counts: int32 [256, 64], P(('expert', 'shard')), may hold values from 0 to 8, as said below
Outputs:
- mixed: bfloat16 [32768, 2048], P(('expert', 'shard'))
Inputs may be any that keep to these rules, and one draw needn't show every extreme that they name: `picks`: within one source device and one expert the 8 entries are different tokens. `counts`: loads differ from expert to expert; in every draw some expert takes 8 tokens from every source device.
All inputs are finite; a program needn't handle non-finite values.
Results may differ from a plain program's by a relative error of at most 0.0057.
Values may be sent and summed in bfloat16 or wider, within the bound.
No kernel may reach another device: no remote copies, remote signals or barrier semaphores. Data moves between devices by JAX's collectives and lax.ppermute only.
A program may use at most 128 MiB of HBM per device.

v0:
```python
import jax
import jax.numpy as jnp
from jax import lax
from jax.experimental import pallas as pl
from jax.experimental.pallas import tpu as pltpu
from jax.sharding import Mesh, PartitionSpec as P

YS, XS, ZS, CS = 4, 4, 8, 2
PLANE = YS * XS
NOTE = 8
NEAR = (0, -1, 1)
FAR = (-2, 2, -3, 3, 4)
ORDER = NEAR + FAR


def shift(block, axis, count, by):
    return lax.ppermute(block, axis, [(i, (i + by) % count) for i in range(count)])


def along_z(block, by):
    return shift(block, "z", ZS, by)


def ring_reduce(part):
    far = ZS // 2
    lines = []
    for half in (0, 1):
        for way in (1, -1):
            last = far if (half == 0) == (way == 1) else far - 1
            lines.append([half, way, last, None])
    for distance in range(far, 0, -1):
        for line in lines:
            half, way, last, moving = line
            if distance > last:
                continue
            mine = part(far if distance == far else way * distance, half)
            if moving is not None:
                mine = mine + moving.astype(jnp.float32)
            line[3] = along_z(mine.astype(jnp.bfloat16), way)
    halves = []
    for half in (0, 1):
        total = part(0, half)
        for line in lines:
            if line[0] == half:
                total = total + line[3].astype(jnp.float32)
        halves.append(total.astype(jnp.bfloat16))
    return jnp.concatenate(halves, axis=0)


def plane_exchange(rows):
    return lax.all_to_all(rows, ("y", "x"), split_axis=0, concat_axis=0, tiled=True)


TRANSPOSED = (((1,), (1,)), ((), ()))


def expert_kernel(column_ref, rows_ref, gate_ref, up_ref, down_ref, out_ref):
    rows = rows_ref[...]
    gate_proj = lax.dot_general(rows, gate_ref[...], TRANSPOSED, preferred_element_type=jnp.float32)
    up_proj = lax.dot_general(rows, up_ref[...], TRANSPOSED, preferred_element_type=jnp.float32)
    lane = lax.broadcasted_iota(jnp.int32, gate_proj.shape, 1)
    logit = jnp.sum(jnp.where(lane == column_ref[0], gate_proj, 0.0), axis=1, keepdims=True)
    weight = 1.0 / (1.0 + jnp.exp(-logit))
    hidden = (gate_proj / (1.0 + jnp.exp(-gate_proj)) * up_proj).astype(jnp.bfloat16)
    out = jnp.dot(hidden, down_ref[...], preferred_element_type=jnp.float32)
    out_ref[...] = (out * weight).astype(out_ref.dtype)


def expert_rows(column, rows, weights, block):
    count, width = rows.shape
    return pl.pallas_call(
        expert_kernel,
        grid=(count // block,),
        in_specs=[
            pl.BlockSpec(memory_space=pltpu.SMEM),
            pl.BlockSpec((block, width), lambda i: (i, 0)),
        ]
        + [pl.BlockSpec(memory_space=pltpu.VMEM)] * len(weights),
        out_specs=pl.BlockSpec((block, width), lambda i: (i, 0)),
        out_shape=jax.ShapeDtypeStruct((count, width), jnp.bfloat16),
        compiler_params=pltpu.CompilerParams(vmem_limit_bytes=28 * 1024 * 1024),
    )(column, rows, *weights)


def shards(tokens, router, w_gate, w_up, w_down, picks, counts):
    tok_count, width = tokens.shape
    half = tok_count // 2
    slots = picks.shape[2]
    zi = lax.axis_index("z")
    pair = zi // 2
    column = (lax.axis_index("y") * XS + lax.axis_index("x")) * (ZS // 2) + pair

    slot_of = lax.broadcasted_iota(jnp.int32, picks.shape[1:], 1)
    code = picks[0] + jnp.where(slot_of < counts[0][:, None], 0, tok_count)
    table = code.reshape(PLANE, ZS // 2, slots).transpose(1, 0, 2).reshape(ZS // 2, PLANE * slots)
    own_codes = lax.dynamic_index_in_dim(table, pair, axis=0, keepdims=False)
    note = jnp.pad(table.astype(jnp.bfloat16), ((0, NOTE - ZS // 2), (0, width - PLANE * slots)))

    first = jnp.concatenate([tokens[:half], note], axis=0)
    lines = {(0, 1): {0: first}, (0, -1): {0: first}, (1, 1): {0: tokens[half:]}, (1, -1): {0: tokens[half:]}}

    def advance(step):
        for (h, way), line in lines.items():
            if step < ZS // 2 or (h == 0) == (way == 1):
                line[step] = along_z(line[step - 1], way)

    def block_of(offset):
        if offset == 0:
            return tokens
        way = 1 if offset < 0 or offset == ZS // 2 else -1
        other = -1 if offset == ZS // 2 else way
        return jnp.concatenate([lines[0, way][abs(offset)][:half], lines[1, other][abs(offset)]], axis=0)

    known = {0: own_codes}

    def codes_of(offset):
        if offset not in known:
            way = 1 if offset < 0 or offset == ZS // 2 else -1
            found = lax.dynamic_slice(lines[0, way][abs(offset)], (half + pair, 0), (1, PLANE * slots))
            known[offset] = found[0].astype(jnp.int32)
        return known[offset]

    def both_cores(own, last):
        return jnp.concatenate([own, shift(own, "c", CS, 1), last], axis=0)

    below = router.T
    weights = (
        both_cores(w_gate[0].T, below),
        both_cores(w_up[0].T, jnp.zeros_like(below)),
        both_cores(w_down[0], jnp.zeros_like(below)),
    )

    token_id = lax.broadcasted_iota(jnp.int32, (1, tok_count), 1)

    def choose(offset):
        index = codes_of(offset) & (tok_count - 1)
        one_hot = (index[:, None] == token_id).astype(jnp.bfloat16)
        rows = jnp.dot(one_hot, block_of(offset), preferred_element_type=jnp.float32)
        return rows.astype(jnp.bfloat16).reshape(PLANE, slots, width)

    def pick_rows(group):
        return jnp.concatenate([choose(o) for o in group], axis=1)

    which = (column + weights[0].shape[0] - below.shape[0]).reshape(1)

    def feed_forward(rows, block):
        return expert_rows(which, rows.reshape(-1, width), weights, block).reshape(rows.shape)

    advance(1)
    advance(2)
    near_rows = plane_exchange(pick_rows(NEAR))
    advance(3)
    advance(4)
    near_rows, far_rows = lax.optimization_barrier((near_rows, pick_rows(FAR)))
    far_rows = plane_exchange(far_rows)
    near_out = feed_forward(near_rows, PLANE * slots * len(NEAR))
    near_out, far_rows = lax.optimization_barrier((near_out, far_rows))
    far_back = plane_exchange(feed_forward(far_rows, PLANE * slots * len(FAR) // 2))
    near_out, far_back = lax.optimization_barrier((near_out, far_back))
    near_back = plane_exchange(near_out)

    kept = lax.optimization_barrier({o: codes_of(o) for o in ORDER})

    def combine(group, rows):
        code = jnp.stack([kept[o].reshape(PLANE, slots) for o in group], axis=1).reshape(1, -1)
        row_of = lax.broadcasted_iota(jnp.int32, (1, code.shape[1]), 1) // slots % len(group)
        place = jnp.where(code < tok_count, code + row_of * tok_count, -1)
        mine = place == lax.broadcasted_iota(jnp.int32, (len(group) * tok_count, 1), 0)
        return jnp.dot(mine.astype(jnp.bfloat16), rows.reshape(-1, width), preferred_element_type=jnp.float32)

    sums = {FAR: combine(FAR, far_back), NEAR: combine(NEAR, near_back)}

    def part(offset, h):
        group = FAR if offset in FAR else NEAR
        start = group.index(offset) * tok_count + h * half
        return sums[group][start : start + half]

    return ring_reduce(part)


def solution(mesh):
    fine = Mesh(mesh.devices.reshape(YS, XS, ZS, CS), ("y", "x", "z", "c"))
    along = ("y", "x", "z")
    placed = (
        P((*along, "c"), None),
        P(),
        P(along, None, "c"),
        P(along, None, "c"),
        P(along, "c", None),
        P((*along, "c"), None, None),
        P((*along, "c"), None),
    )
    return jax.shard_map(
        shards, mesh=fine, in_specs=placed, out_specs=P((*along, "c"), None), check_vma=False
    )
```

profile of v0, /device:TPU:32, one launch (start us, length us, event | category | flops | bytes accessed | tf_op | source)
XLA Modules:
  0.0 220.6 jit_solution(3577966785089433493)
XLA Ops:
  2.4 1.3 reduce.3
  4.0 2.0 collective-permute-start
  6.1 1.9 collective-permute-start.7
  8.0 2.1 collective-permute-start.8
  10.1 1.4 fusion
  11.5 6.9 %collective-permute-done.7 = bf16[64,2048]{1,0:T(8,128)(2,1)S(1)} collective-permute-done((bf16[64,2048]{1,0:T(8,128)(2,1)S(1)}, bf16[64,2048]{1,0:T(8,128)(2,1)S(1)}, u32[]{:S(2)}, u32[]{:S(2)}) %collective-permute-start.7) | collective-permute-done | bytes 262176 | tf_op jit(solution)/shard_map/ppermute | solution.py:17
  18.4 1.9 collective-permute-start.9
  20.4 2.3 %collective-permute-start.10 = (bf16[64,2048]{1,0:T(8,128)(2,1)S(1)}, bf16[64,2048]{1,0:T(8,128)(2,1)}, u32[]{:S(2)}, u32[]{:S(2)}) collective-permute-start(bf16[64,2048]{1,0:T(8,128)(2,1)S(1)} %collective-permute-done.8), channel_id=1, source_target_pairs={{0,14},{2,0},{4,2},{6,4},{8,6},{10,8},{12,10},{14,12},{1,15},{3,1}... | collective-permute-start | bytes 786440 | tf_op jit(solution)/shard_map/ppermute | solution.py:17
  23.4 2.6 %collective-permute-start.4 = (bf16[72,2048]{1,0:T(8,128)(2,1)S(1)}, bf16[72,2048]{1,0:T(8,128)(2,1)S(1)}, u32[]{:S(2)}, u32[]{:S(2)}) collective-permute-start(bf16[72,2048]{1,0:T(8,128)(2,1)S(1)} %collective-permute-done.3), channel_id=1, source_target_pairs={{0,14},{2,0},{4,2},{6,4},{8,6},{10,8},{12,10},{14,12},{1,15},{3,1}... | collective-permute-start | bytes 884744 | tf_op jit(solution)/shard_map/ppermute | solution.py:17
  28.1 7.0 %all-to-all-start = ((bf16[16,24,2048]{2,1,0:T(8,128)(2,1)}), bf16[16,24,2048]{2,1,0:T(8,128)(2,1)S(1)}, u32[]{:S(2)}, u32[]{:S(2)}) async-start(bf16[16,24,2048]{2,1,0:T(8,128)(2,1)} %pad_maximum_fusion.1), calls=%async_computation | async-start | bytes 3145728 | tf_op jit(solution)/shard_map/all_to_all | solution.py:51
  35.9 2.5 %collective-permute-start.12 = (bf16[64,2048]{1,0:T(8,128)(2,1)}, bf16[64,2048]{1,0:T(8,128)(2,1)S(1)}, u32[]{:S(2)}, u32[]{:S(2)}) collective-permute-start(bf16[64,2048]{1,0:T(8,128)(2,1)} %collective-permute-done.10), channel_id=1, source_target_pairs={{0,14},{2,0},{4,2},{6,4},{8,6},{10,8},{12,10},{14,12},{1,15},{3,1}... | collective-permute-start | bytes 786440 | tf_op jit(solution)/shard_map/ppermute | solution.py:17
  39.2 2.5 %collective-permute-start.5 = (bf16[72,2048]{1,0:T(8,128)(2,1)S(1)}, bf16[72,2048]{1,0:T(8,128)(2,1)S(1)}, u32[]{:S(2)}, u32[]{:S(2)}) collective-permute-start(bf16[72,2048]{1,0:T(8,128)(2,1)S(1)} %collective-permute-done.4), channel_id=1, source_target_pairs={{0,14},{2,0},{4,2},{6,4},{8,6},{10,8},{12,10},{14,12},{1,15},{3,1}... | collective-permute-start | bytes 884744 | tf_op jit(solution)/shard_map/ppermute | solution.py:17
  41.7 2.1 fusion.4
  43.9 2.1 fusion.6
  46.5 2.7 %collective-permute-start.13 = (bf16[64,2048]{1,0:T(8,128)(2,1)S(1)}, bf16[64,2048]{1,0:T(8,128)(2,1)S(1)}, u32[]{:S(2)}, u32[]{:S(2)}) collective-permute-start(bf16[64,2048]{1,0:T(8,128)(2,1)S(1)} %collective-permute-done.12), channel_id=1, source_target_pairs={{0,14},{2,0},{4,2},{6,4},{8,6},{10,8},{12,10},{14,12},{1,15},{3,1}... | collective-permute-start | bytes 786440 | tf_op jit(solution)/shard_map/ppermute | solution.py:17
  50.0 2.4 %collective-permute-done.5 = bf16[72,2048]{1,0:T(8,128)(2,1)S(1)} collective-permute-done((bf16[72,2048]{1,0:T(8,128)(2,1)S(1)}, bf16[72,2048]{1,0:T(8,128)(2,1)S(1)}, u32[]{:S(2)}, u32[]{:S(2)}) %collective-permute-start.5) | collective-permute-done | bytes 294944 | tf_op jit(solution)/shard_map/ppermute | solution.py:17
  54.8 2.4 %collective-permute-done.6 = bf16[72,2048]{1,0:T(8,128)(2,1)S(1)} collective-permute-done((bf16[72,2048]{1,0:T(8,128)(2,1)S(1)}, bf16[72,2048]{1,0:T(8,128)(2,1)S(1)}, u32[]{:S(2)}, u32[]{:S(2)}) %collective-permute-start.6) | collective-permute-done | bytes 294944 | tf_op jit(solution)/shard_map/ppermute | solution.py:17
  58.4 7.5 %all-to-all-start.1 = ((bf16[16,40,2048]{2,1,0:T(8,128)(2,1)}), bf16[16,40,2048]{2,1,0:T(8,128)(2,1)}, u32[]{:S(2)}, u32[]{:S(2)}) async-start(bf16[16,40,2048]{2,1,0:T(8,128)(2,1)} %fusion.12), calls=%async_computation.1 | async-start | bytes 5242880 | tf_op jit(solution)/shard_map/all_to_all | solution.py:51
  66.7 3.7 %collective-permute-done.14 = bf16[352,2048]{1,0:T(8,128)(2,1)} collective-permute-done((bf16[352,2048]{1,0:T(8,128)(2,1)S(1)}, bf16[352,2048]{1,0:T(8,128)(2,1)}, u32[]{:S(2)}, u32[]{:S(2)}) %collective-permute-start.14) | collective-permute-done | bytes 1441824 | tf_op jit(solution)/shard_map/ppermute | solution.py:17
  70.4 1.9 pad_maximum_fusion.gate_ref
  72.4 1.3 collective-permute-done.16
  73.7 3.2 %maximum_maximum_fusion.1 = (bf16[768,2048]{1,0:T(8,128)(2,1)S(1)}, bf16[768,2048]{1,0:T(8,128)(2,1)S(1)}) fusion(bf16[352,2048]{1,0:T(8,128)(2,1)} %collective-permute-done.16, bf16[352,2048]{1,0:T(8,128)(2,1)} %bitcast.34, bf16[768]{0:T(1024)(128)(2,1)S(1)} %pad.12.clone, bf16[352,2048]{1,0:T(8,128)(2,1)} %collective-permute-done.15, ...), kind=kLoop, calls=%fused_computation.2 | loop fusion | flops 17301504 | bytes 12060160 | tf_op jit(solution)/shard_map/concatenate | solution.py:124
  76.9 5.1 %shard_map.73 = bf16[384,2048]{1,0:T(8,128)(2,1)} custom-call(s32[1]{0:T(128)} %bitcast.10.column_ref, bf16[384,2048]{1,0:T(8,128)(2,1)S(1)} %bitcast.93, bf16[768,2048]{1,0:T(8,128)(2,1)S(1)} %pad_maximum_fusion.gate_ref, bf16[768,2048]{1,0:T(8,128)(2,1)S(1)} %get-tuple-element.65.up_ref, bf16[768,2048]{1,0:T(8,128)(2,1)S(1)} %get-tuple-element.64.down_ref), custom_call_target="tpu_custom_call" | custom-call | tf_op jit(solution)/shard_map/pallas_call | solution.py:71
  82.0 1.7 copy-done
  83.7 1.6 copy-done.2
  85.3 13.5 %all-to-all-done.1 = bf16[16,40,2048]{2,1,0:T(8,128)(2,1)} async-done(((bf16[16,40,2048]{2,1,0:T(8,128)(2,1)}), bf16[16,40,2048]{2,1,0:T(8,128)(2,1)}, u32[]{:S(2)}, u32[]{:S(2)}) %all-to-all-start.1) | async-done | bytes 2621472 | tf_op jit(solution)/shard_map/all_to_all | solution.py:51
  98.8 1.9 copy-done.1
  100.7 1.9 copy-done.3
  102.6 7.9 %shard_map.74 = bf16[640,2048]{1,0:T(8,128)(2,1)S(1)} custom-call(s32[1]{0:T(128)} %bitcast.10.column_ref, bf16[640,2048]{1,0:T(8,128)(2,1)} %bitcast.36.rows_ref, bf16[768,2048]{1,0:T(8,128)(2,1)S(1)} %pad_maximum_fusion.gate_ref, bf16[768,2048]{1,0:T(8,128)(2,1)S(1)} %copy-done.3, bf16[768,2048]{1,0:T(8,128)(2,1)S(1)} %copy-done.1), custom_call_target="tpu_custom_call" | custom-call | tf_op jit(solution)/shard_map/pallas_call | solution.py:71
  110.5 1.5 copy-done.4
  112.0 14.1 %all-to-all-start.2 = ((bf16[16,40,2048]{2,1,0:T(8,128)(2,1)}), bf16[16,40,2048]{2,1,0:T(8,128)(2,1)S(1)}, u32[]{:S(2)}, u32[]{:S(2)}) async-start(bf16[16,40,2048]{2,1,0:T(8,128)(2,1)} %bitcast.92), calls=%async_computation.2 | async-start | bytes 5242880 | tf_op jit(solution)/shard_map/all_to_all | solution.py:51
  126.7 34.2 %all-to-all-done.2 = bf16[16,40,2048]{2,1,0:T(8,128)(2,1)S(1)} async-done(((bf16[16,40,2048]{2,1,0:T(8,128)(2,1)}), bf16[16,40,2048]{2,1,0:T(8,128)(2,1)S(1)}, u32[]{:S(2)}, u32[]{:S(2)}) %all-to-all-start.2) | async-done | bytes 2621472 | tf_op jit(solution)/shard_map/all_to_all | solution.py:51
  161.0 2.2 fusion.111
  164.1 1.3 collective-permute-start.17
  166.1 1.8 collective-permute-start.24
  168.2 4.2 %collective-permute-done.17 = bf16[64,2048]{1,0:T(8,128)(2,1)S(1)} collective-permute-done((bf16[64,2048]{1,0:T(8,128)(2,1)S(1)}, bf16[64,2048]{1,0:T(8,128)(2,1)S(1)}, u32[]{:S(2)}, u32[]{:S(2)}) %collective-permute-start.17) | collective-permute-done | bytes 262176 | tf_op jit(solution)/shard_map/ppermute | solution.py:17
  172.4 2.4 %collective-permute-start.18 = (bf16[64,2048]{1,0:T(8,128)(2,1)S(1)}, bf16[64,2048]{1,0:T(8,128)(2,1)S(1)}, u32[]{:S(2)}, u32[]{:S(2)}) collective-permute-start(bf16[64,2048]{1,0:T(8,128)(2,1)S(1)} %fusion.26), channel_id=1, source_target_pairs={{0,2},{2,4},{4,6},{6,8},{8,10},{10,12},{12,14},{14,0},{1,3},{3,5},... | collective-permute-start | bytes 786440 | tf_op jit(solution)/shard_map/ppermute | solution.py:17
  174.8 3.7 %all-to-all-start.3 = ((bf16[16,24,2048]{2,1,0:T(8,128)(2,1)}), bf16[16,24,2048]{2,1,0:T(8,128)(2,1)S(1)}, u32[]{:S(2)}, u32[]{:S(2)}) async-start(bf16[16,24,2048]{2,1,0:T(8,128)(2,1)} %bitcast.35), calls=%async_computation.3 | async-start | bytes 3145728 | tf_op jit(solution)/shard_map/all_to_all | solution.py:51
  179.8 2.5 %fusion.27 = (bf16[64,2048]{1,0:T(8,128)(2,1)S(1)}, bf16[64,2048]{1,0:T(8,128)(2,1)}, bf16[64,2048]{1,0:T(8,128)(2,1)S(1)}, bf16[64,2048]{1,0:T(8,128)(2,1)S(1)}) fusion(f32[640,2048]{1,0:T(8,128)} %copy-done.7, bf16[64,2048]{1,0:T(8,128)(2,1)S(1)} %collective-permute-done.18, bf16[64,2048]{1,0:T(8,128)(2,1)S(1)} %collective-permute-done.27, ...), kind=kLoop, calls=%fused_computation.52 | loop fusion | flops 1572864 | bytes 4194304 | tf_op jit(solution)/shard_map/convert_element_type | solution.py:39
  182.3 3.2 %collective-permute-start.28 = (bf16[64,2048]{1,0:T(8,128)(2,1)}, bf16[64,2048]{1,0:T(8,128)(2,1)S(1)}, u32[]{:S(2)}, u32[]{:S(2)}) collective-permute-start(bf16[64,2048]{1,0:T(8,128)(2,1)} %get-tuple-element.50), channel_id=1, source_target_pairs={{0,14},{2,0},{4,2},{6,4},{8,6},{10,8},{12,10},{14,12},{1,15},{3,1}... | collective-permute-start | bytes 786440 | tf_op jit(solution)/shard_map/ppermute | solution.py:17
  185.8 2.0 collective-permute-start.22
  187.9 4.1 %collective-permute-done.28 = bf16[64,2048]{1,0:T(8,128)(2,1)S(1)} collective-permute-done((bf16[64,2048]{1,0:T(8,128)(2,1)}, bf16[64,2048]{1,0:T(8,128)(2,1)S(1)}, u32[]{:S(2)}, u32[]{:S(2)}) %collective-permute-start.28) | collective-permute-done | bytes 262176 | tf_op jit(solution)/shard_map/ppermute | solution.py:17
  193.0 2.5 %collective-permute-start.29 = (bf16[64,2048]{1,0:T(8,128)(2,1)S(1)}, bf16[64,2048]{1,0:T(8,128)(2,1)S(1)}, u32[]{:S(2)}, u32[]{:S(2)}) collective-permute-start(bf16[64,2048]{1,0:T(8,128)(2,1)S(1)} %fusion.18), channel_id=1, source_target_pairs={{0,14},{2,0},{4,2},{6,4},{8,6},{10,8},{12,10},{14,12},{1,15},{3,1}... | collective-permute-start | bytes 786440 | tf_op jit(solution)/shard_map/ppermute | solution.py:17
  195.5 4.3 %all-to-all-done.3 = bf16[16,24,2048]{2,1,0:T(8,128)(2,1)S(1)} async-done(((bf16[16,24,2048]{2,1,0:T(8,128)(2,1)}), bf16[16,24,2048]{2,1,0:T(8,128)(2,1)S(1)}, u32[]{:S(2)}, u32[]{:S(2)}) %all-to-all-start.3) | async-done | bytes 1572896 | tf_op jit(solution)/shard_map/all_to_all | solution.py:51
  201.9 2.6 %collective-permute-start.20 = (bf16[64,2048]{1,0:T(8,128)(2,1)S(1)}, bf16[64,2048]{1,0:T(8,128)(2,1)S(1)}, u32[]{:S(2)}, u32[]{:S(2)}) collective-permute-start(bf16[64,2048]{1,0:T(8,128)(2,1)S(1)} %get-tuple-element.56), channel_id=1, source_target_pairs={{0,2},{2,4},{4,6},{6,8},{8,10},{10,12},{12,14},{14,0},{1,3},{3,5},... | collective-permute-start | bytes 786440 | tf_op jit(solution)/shard_map/ppermute | solution.py:17
  204.5 4.7 %collective-permute-done.20 = bf16[64,2048]{1,0:T(8,128)(2,1)S(1)} collective-permute-done((bf16[64,2048]{1,0:T(8,128)(2,1)S(1)}, bf16[64,2048]{1,0:T(8,128)(2,1)S(1)}, u32[]{:S(2)}, u32[]{:S(2)}) %collective-permute-start.20) | collective-permute-done | bytes 262176 | tf_op jit(solution)/shard_map/ppermute | solution.py:17
  209.2 2.7 %collective-permute-done.23 = bf16[64,2048]{1,0:T(8,128)(2,1)S(1)} collective-permute-done((bf16[64,2048]{1,0:T(8,128)(2,1)S(1)}, bf16[64,2048]{1,0:T(8,128)(2,1)S(1)}, u32[]{:S(2)}, u32[]{:S(2)}) %collective-permute-start.23) | collective-permute-done | bytes 262176 | tf_op jit(solution)/shard_map/ppermute | solution.py:17
  214.2 4.3 %collective-permute-done.26 = bf16[64,2048]{1,0:T(8,128)(2,1)S(1)} collective-permute-done((bf16[64,2048]{1,0:T(8,128)(2,1)S(1)}, bf16[64,2048]{1,0:T(8,128)(2,1)S(1)}, u32[]{:S(2)}, u32[]{:S(2)}) %collective-permute-start.26) | collective-permute-done | bytes 262176 | tf_op jit(solution)/shard_map/ppermute | solution.py:17
  (112 shorter events, 24.2 us)
Async XLA Ops:
  4.0 18.7 %collective-permute-start = (bf16[72,2048]{1,0:T(8,128)(2,1)S(1)}, bf16[72,2048]{1,0:T(8,128)(2,1)S(1)}, u32[]{:S(2)}, u32[]{:S(2)}) collective-permute-start(bf16[72,2048]{1,0:T(8,128)(2,1)S(1)} %fusion.52), channel_id=1, source_target_pairs={{0,2},{2,4},{4,6},{6,8},{8,10},{10,12},{12,14},{14,0},{1,3},{3,5},... | collective-permute-start | bytes 884744 | tf_op jit(solution)/shard_map/ppermute | solution.py:17
  6.0 17.4 %collective-permute-start.3 = (bf16[72,2048]{1,0:T(8,128)(2,1)S(1)}, bf16[72,2048]{1,0:T(8,128)(2,1)S(1)}, u32[]{:S(2)}, u32[]{:S(2)}) collective-permute-start(bf16[72,2048]{1,0:T(8,128)(2,1)S(1)} %fusion.52), channel_id=1, source_target_pairs={{0,14},{2,0},{4,2},{6,4},{8,6},{10,8},{12,10},{14,12},{1,15},{3,1}... | collective-permute-start | bytes 884744 | tf_op jit(solution)/shard_map/ppermute | solution.py:17
  6.1 12.3 %collective-permute-start.7 = (bf16[64,2048]{1,0:T(8,128)(2,1)S(1)}, bf16[64,2048]{1,0:T(8,128)(2,1)S(1)}, u32[]{:S(2)}, u32[]{:S(2)}) collective-permute-start(bf16[64,2048]{1,0:T(8,128)(2,1)S(1)} %get-tuple-element.63), channel_id=1, source_target_pairs={{0,2},{2,4},{4,6},{6,8},{8,10},{10,12},{12,14},{14,0},{1,3},{3,5},... | collective-permute-start | bytes 786440 | tf_op jit(solution)/shard_map/ppermute | solution.py:17
  8.0 12.3 %collective-permute-start.8 = (bf16[64,2048]{1,0:T(8,128)(2,1)S(1)}, bf16[64,2048]{1,0:T(8,128)(2,1)S(1)}, u32[]{:S(2)}, u32[]{:S(2)}) collective-permute-start(bf16[64,2048]{1,0:T(8,128)(2,1)S(1)} %get-tuple-element.63), channel_id=1, source_target_pairs={{0,14},{2,0},{4,2},{6,4},{8,6},{10,8},{12,10},{14,12},{1,15},{3,1}... | collective-permute-start | bytes 786440 | tf_op jit(solution)/shard_map/ppermute | solution.py:17
  18.4 16.7 %collective-permute-start.9 = (bf16[64,2048]{1,0:T(8,128)(2,1)S(1)}, bf16[64,2048]{1,0:T(8,128)(2,1)}, u32[]{:S(2)}, u32[]{:S(2)}) collective-permute-start(bf16[64,2048]{1,0:T(8,128)(2,1)S(1)} %collective-permute-done.7), channel_id=1, source_target_pairs={{0,2},{2,4},{4,6},{6,8},{8,10},{10,12},{12,14},{14,0},{1,3},{3,5},... | collective-permute-start | bytes 786440 | tf_op jit(solution)/shard_map/ppermute | solution.py:17
  20.4 15.6 %collective-permute-start.10 = (bf16[64,2048]{1,0:T(8,128)(2,1)S(1)}, bf16[64,2048]{1,0:T(8,128)(2,1)}, u32[]{:S(2)}, u32[]{:S(2)}) collective-permute-start(bf16[64,2048]{1,0:T(8,128)(2,1)S(1)} %collective-permute-done.8), channel_id=1, source_target_pairs={{0,14},{2,0},{4,2},{6,4},{8,6},{10,8},{12,10},{14,12},{1,15},{3,1}... | collective-permute-start | bytes 786440 | tf_op jit(solution)/shard_map/ppermute | solution.py:17
  22.7 15.8 %collective-permute-start.1 = (bf16[72,2048]{1,0:T(8,128)(2,1)S(1)}, bf16[72,2048]{1,0:T(8,128)(2,1)S(1)}, u32[]{:S(2)}, u32[]{:S(2)}) collective-permute-start(bf16[72,2048]{1,0:T(8,128)(2,1)S(1)} %collective-permute-done), channel_id=1, source_target_pairs={{0,2},{2,4},{4,6},{6,8},{8,10},{10,12},{12,14},{14,0},{1,3},{3,5},... | collective-permute-start | bytes 884744 | tf_op jit(solution)/shard_map/ppermute | solution.py:17
  23.4 15.8 %collective-permute-start.4 = (bf16[72,2048]{1,0:T(8,128)(2,1)S(1)}, bf16[72,2048]{1,0:T(8,128)(2,1)S(1)}, u32[]{:S(2)}, u32[]{:S(2)}) collective-permute-start(bf16[72,2048]{1,0:T(8,128)(2,1)S(1)} %collective-permute-done.3), channel_id=1, source_target_pairs={{0,14},{2,0},{4,2},{6,4},{8,6},{10,8},{12,10},{14,12},{1,15},{3,1}... | collective-permute-start | bytes 884744 | tf_op jit(solution)/shard_map/ppermute | solution.py:17
  28.1 30.3 %all-to-all-start = ((bf16[16,24,2048]{2,1,0:T(8,128)(2,1)}), bf16[16,24,2048]{2,1,0:T(8,128)(2,1)S(1)}, u32[]{:S(2)}, u32[]{:S(2)}) async-start(bf16[16,24,2048]{2,1,0:T(8,128)(2,1)} %pad_maximum_fusion.1), calls=%async_computation | async-start | bytes 3145728 | tf_op jit(solution)/shard_map/all_to_all | solution.py:51
  35.1 17.4 %collective-permute-start.11 = (bf16[64,2048]{1,0:T(8,128)(2,1)}, bf16[64,2048]{1,0:T(8,128)(2,1)S(1)}, u32[]{:S(2)}, u32[]{:S(2)}) collective-permute-start(bf16[64,2048]{1,0:T(8,128)(2,1)} %collective-permute-done.9), channel_id=1, source_target_pairs={{0,2},{2,4},{4,6},{6,8},{8,10},{10,12},{12,14},{14,0},{1,3},{3,5},... | collective-permute-start | bytes 786440 | tf_op jit(solution)/shard_map/ppermute | solution.py:17
  35.9 10.6 %collective-permute-start.12 = (bf16[64,2048]{1,0:T(8,128)(2,1)}, bf16[64,2048]{1,0:T(8,128)(2,1)S(1)}, u32[]{:S(2)}, u32[]{:S(2)}) collective-permute-start(bf16[64,2048]{1,0:T(8,128)(2,1)} %collective-permute-done.10), channel_id=1, source_target_pairs={{0,14},{2,0},{4,2},{6,4},{8,6},{10,8},{12,10},{14,12},{1,15},{3,1}... | collective-permute-start | bytes 786440 | tf_op jit(solution)/shard_map/ppermute | solution.py:17
  38.4 10.8 %collective-permute-start.2 = (bf16[72,2048]{1,0:T(8,128)(2,1)S(1)}, bf16[72,2048]{1,0:T(8,128)(2,1)S(1)}, u32[]{:S(2)}, u32[]{:S(2)}) collective-permute-start(bf16[72,2048]{1,0:T(8,128)(2,1)S(1)} %collective-permute-done.1), channel_id=1, source_target_pairs={{0,2},{2,4},{4,6},{6,8},{8,10},{10,12},{12,14},{14,0},{1,3},{3,5},... | collective-permute-start | bytes 884744 | tf_op jit(solution)/shard_map/ppermute | solution.py:17
  39.2 13.2 %collective-permute-start.5 = (bf16[72,2048]{1,0:T(8,128)(2,1)S(1)}, bf16[72,2048]{1,0:T(8,128)(2,1)S(1)}, u32[]{:S(2)}, u32[]{:S(2)}) collective-permute-start(bf16[72,2048]{1,0:T(8,128)(2,1)S(1)} %collective-permute-done.4), channel_id=1, source_target_pairs={{0,14},{2,0},{4,2},{6,4},{8,6},{10,8},{12,10},{14,12},{1,15},{3,1}... | collective-permute-start | bytes 884744 | tf_op jit(solution)/shard_map/ppermute | solution.py:17
  46.5 10.7 %collective-permute-start.13 = (bf16[64,2048]{1,0:T(8,128)(2,1)S(1)}, bf16[64,2048]{1,0:T(8,128)(2,1)S(1)}, u32[]{:S(2)}, u32[]{:S(2)}) collective-permute-start(bf16[64,2048]{1,0:T(8,128)(2,1)S(1)} %collective-permute-done.12), channel_id=1, source_target_pairs={{0,14},{2,0},{4,2},{6,4},{8,6},{10,8},{12,10},{14,12},{1,15},{3,1}... | collective-permute-start | bytes 786440 | tf_op jit(solution)/shard_map/ppermute | solution.py:17
  49.2 8.0 %collective-permute-start.6 = (bf16[72,2048]{1,0:T(8,128)(2,1)S(1)}, bf16[72,2048]{1,0:T(8,128)(2,1)S(1)}, u32[]{:S(2)}, u32[]{:S(2)}) collective-permute-start(bf16[72,2048]{1,0:T(8,128)(2,1)S(1)} %collective-permute-done.2), channel_id=1, source_target_pairs={{0,2},{2,4},{4,6},{6,8},{8,10},{10,12},{12,14},{14,0},{1,3},{3,5},... | collective-permute-start | bytes 884744 | tf_op jit(solution)/shard_map/ppermute | solution.py:17
  58.4 7.6 %copy-start.8 = (bf16[1,2048,352]{1,2,0:T(8,128)(2,1)S(1)}, bf16[1,2048,352]{1,2,0:T(8,128)(2,1)}, u32[]{:S(2)}) copy-start(bf16[1,2048,352]{1,2,0:T(8,128)(2,1)} %param.9) | copy-start | bytes 4325380
  58.4 12.1 %copy-start.9 = (bf16[2048,64]{0,1:T(8,128)(2,1)S(1)}, bf16[2048,64]{0,1:T(8,128)(2,1)}, u32[]{:S(2)}) copy-start(bf16[2048,64]{0,1:T(8,128)(2,1)} %param.8) | copy-start | bytes 786436
  58.4 7.5 %copy-start.5 = (bf16[16,24,2048]{2,1,0:T(8,128)(2,1)}, bf16[16,24,2048]{2,1,0:T(8,128)(2,1)S(1)}, u32[]{:S(2)}) copy-start(bf16[16,24,2048]{2,1,0:T(8,128)(2,1)S(1)} %all-to-all-done) | copy-start | bytes 4718596
  58.4 40.4 %all-to-all-start.1 = ((bf16[16,40,2048]{2,1,0:T(8,128)(2,1)}), bf16[16,40,2048]{2,1,0:T(8,128)(2,1)}, u32[]{:S(2)}, u32[]{:S(2)}) async-start(bf16[16,40,2048]{2,1,0:T(8,128)(2,1)} %fusion.12), calls=%async_computation.1 | async-start | bytes 5242880 | tf_op jit(solution)/shard_map/all_to_all | solution.py:51
  66.0 4.5 %collective-permute-start.14 = (bf16[352,2048]{1,0:T(8,128)(2,1)S(1)}, bf16[352,2048]{1,0:T(8,128)(2,1)}, u32[]{:S(2)}, u32[]{:S(2)}) collective-permute-start(bf16[352,2048]{1,0:T(8,128)(2,1)S(1)} %bitcast.97), channel_id=1, source_target_pairs={{0,1},{1,0},{2,3},{3,2},{4,5},{5,4},{6,7},{7,6},{8,9},{9,8},{10,11... | collective-permute-start | bytes 4325384 | tf_op jit(solution)/shard_map/ppermute | solution.py:17
  66.1 6.4 %collective-permute-start.15 = (bf16[352,2048]{1,0:T(8,128)(2,1)}, bf16[352,2048]{1,0:T(8,128)(2,1)}, u32[]{:S(2)}, u32[]{:S(2)}) collective-permute-start(bf16[352,2048]{1,0:T(8,128)(2,1)} %bitcast.32), channel_id=1, source_target_pairs={{0,1},{1,0},{2,3},{3,2},{4,5},{5,4},{6,7},{7,6},{8,9},{9,8},{10,11... | collective-permute-start | bytes 4325384 | tf_op jit(solution)/shard_map/ppermute | solution.py:17
  66.6 7.2 %collective-permute-start.16 = (bf16[352,2048]{1,0:T(8,128)(2,1)}, bf16[352,2048]{1,0:T(8,128)(2,1)}, u32[]{:S(2)}, u32[]{:S(2)}) collective-permute-start(bf16[352,2048]{1,0:T(8,128)(2,1)} %bitcast.34), channel_id=1, source_target_pairs={{0,1},{1,0},{2,3},{3,2},{4,5},{5,4},{6,7},{7,6},{8,9},{9,8},{10,11... | collective-permute-start | bytes 4325384 | tf_op jit(solution)/shard_map/ppermute | solution.py:17
  72.4 4.5 %copy-start.6 = (bf16[16,24,2048]{2,1,0:T(8,128)(2,1)S(1)}, bf16[16,24,2048]{2,1,0:T(8,128)(2,1)}, u32[]{:S(2)}) copy-start(bf16[16,24,2048]{2,1,0:T(8,128)(2,1)} %copy-done.5) | copy-start | bytes 4718596
  82.0 1.7 copy-start
  83.7 1.6 copy-start.2
  98.8 1.9 copy-start.1
  100.7 1.9 copy-start.3
  110.5 1.5 copy-start.4
  112.0 49.0 %all-to-all-start.2 = ((bf16[16,40,2048]{2,1,0:T(8,128)(2,1)}), bf16[16,40,2048]{2,1,0:T(8,128)(2,1)S(1)}, u32[]{:S(2)}, u32[]{:S(2)}) async-start(bf16[16,40,2048]{2,1,0:T(8,128)(2,1)} %bitcast.92), calls=%async_computation.2 | async-start | bytes 5242880 | tf_op jit(solution)/shard_map/all_to_all | solution.py:51
  163.2 9.2 %copy-start.7 = (f32[640,2048]{1,0:T(8,128)}, f32[640,2048]{1,0:T(8,128)S(1)}, u32[]{:S(2)}) copy-start(f32[640,2048]{1,0:T(8,128)S(1)} %get-tuple-element.67) | copy-start | bytes 15728644
  164.1 8.3 %collective-permute-start.17 = (bf16[64,2048]{1,0:T(8,128)(2,1)S(1)}, bf16[64,2048]{1,0:T(8,128)(2,1)S(1)}, u32[]{:S(2)}, u32[]{:S(2)}) collective-permute-start(bf16[64,2048]{1,0:T(8,128)(2,1)S(1)} %get-tuple-element.58), channel_id=1, source_target_pairs={{0,2},{2,4},{4,6},{6,8},{8,10},{10,12},{12,14},{14,0},{1,3},{3,5},... | collective-permute-start | bytes 786440 | tf_op jit(solution)/shard_map/ppermute | solution.py:17
  165.4 13.4 %collective-permute-start.21 = (bf16[64,2048]{1,0:T(8,128)(2,1)}, bf16[64,2048]{1,0:T(8,128)(2,1)S(1)}, u32[]{:S(2)}, u32[]{:S(2)}) collective-permute-start(bf16[64,2048]{1,0:T(8,128)(2,1)} %get-tuple-element.61), channel_id=1, source_target_pairs={{0,14},{2,0},{4,2},{6,4},{8,6},{10,8},{12,10},{14,12},{1,15},{3,1}... | collective-permute-start | bytes 786440 | tf_op jit(solution)/shard_map/ppermute | solution.py:17
  166.1 12.6 %collective-permute-start.24 = (bf16[64,2048]{1,0:T(8,128)(2,1)S(1)}, bf16[64,2048]{1,0:T(8,128)(2,1)S(1)}, u32[]{:S(2)}, u32[]{:S(2)}) collective-permute-start(bf16[64,2048]{1,0:T(8,128)(2,1)S(1)} %get-tuple-element.60), channel_id=1, source_target_pairs={{0,2},{2,4},{4,6},{6,8},{8,10},{10,12},{12,14},{14,0},{1,3},{3,5},... | collective-permute-start | bytes 786440 | tf_op jit(solution)/shard_map/ppermute | solution.py:17
  167.9 10.9 %collective-permute-start.27 = (bf16[64,2048]{1,0:T(8,128)(2,1)S(1)}, bf16[64,2048]{1,0:T(8,128)(2,1)S(1)}, u32[]{:S(2)}, u32[]{:S(2)}) collective-permute-start(bf16[64,2048]{1,0:T(8,128)(2,1)S(1)} %get-tuple-element.59), channel_id=1, source_target_pairs={{0,14},{2,0},{4,2},{6,4},{8,6},{10,8},{12,10},{14,12},{1,15},{3,1}... | collective-permute-start | bytes 786440 | tf_op jit(solution)/shard_map/ppermute | solution.py:17
  172.4 7.4 %collective-permute-start.18 = (bf16[64,2048]{1,0:T(8,128)(2,1)S(1)}, bf16[64,2048]{1,0:T(8,128)(2,1)S(1)}, u32[]{:S(2)}, u32[]{:S(2)}) collective-permute-start(bf16[64,2048]{1,0:T(8,128)(2,1)S(1)} %fusion.26), channel_id=1, source_target_pairs={{0,2},{2,4},{4,6},{6,8},{8,10},{10,12},{12,14},{14,0},{1,3},{3,5},... | collective-permute-start | bytes 786440 | tf_op jit(solution)/shard_map/ppermute | solution.py:17
  174.8 25.0 %all-to-all-start.3 = ((bf16[16,24,2048]{2,1,0:T(8,128)(2,1)}), bf16[16,24,2048]{2,1,0:T(8,128)(2,1)S(1)}, u32[]{:S(2)}, u32[]{:S(2)}) async-start(bf16[16,24,2048]{2,1,0:T(8,128)(2,1)} %bitcast.35), calls=%async_computation.3 | async-start | bytes 3145728 | tf_op jit(solution)/shard_map/all_to_all | solution.py:51
  182.3 9.6 %collective-permute-start.28 = (bf16[64,2048]{1,0:T(8,128)(2,1)}, bf16[64,2048]{1,0:T(8,128)(2,1)S(1)}, u32[]{:S(2)}, u32[]{:S(2)}) collective-permute-start(bf16[64,2048]{1,0:T(8,128)(2,1)} %get-tuple-element.50), channel_id=1, source_target_pairs={{0,14},{2,0},{4,2},{6,4},{8,6},{10,8},{12,10},{14,12},{1,15},{3,1}... | collective-permute-start | bytes 786440 | tf_op jit(solution)/shard_map/ppermute | solution.py:17
  185.7 15.1 %collective-permute-start.19 = (bf16[64,2048]{1,0:T(8,128)(2,1)S(1)}, bf16[64,2048]{1,0:T(8,128)(2,1)S(1)}, u32[]{:S(2)}, u32[]{:S(2)}) collective-permute-start(bf16[64,2048]{1,0:T(8,128)(2,1)S(1)} %get-tuple-element.49), channel_id=1, source_target_pairs={{0,2},{2,4},{4,6},{6,8},{8,10},{10,12},{12,14},{14,0},{1,3},{3,5},... | collective-permute-start | bytes 786440 | tf_op jit(solution)/shard_map/ppermute | solution.py:17
  185.8 15.0 %collective-permute-start.22 = (bf16[64,2048]{1,0:T(8,128)(2,1)S(1)}, bf16[64,2048]{1,0:T(8,128)(2,1)}, u32[]{:S(2)}, u32[]{:S(2)}) collective-permute-start(bf16[64,2048]{1,0:T(8,128)(2,1)S(1)} %get-tuple-element.52), channel_id=1, source_target_pairs={{0,14},{2,0},{4,2},{6,4},{8,6},{10,8},{12,10},{14,12},{1,15},{3,1}... | collective-permute-start | bytes 786440 | tf_op jit(solution)/shard_map/ppermute | solution.py:17
  187.8 16.7 %collective-permute-start.25 = (bf16[64,2048]{1,0:T(8,128)(2,1)S(1)}, bf16[64,2048]{1,0:T(8,128)(2,1)S(1)}, u32[]{:S(2)}, u32[]{:S(2)}) collective-permute-start(bf16[64,2048]{1,0:T(8,128)(2,1)S(1)} %get-tuple-element.51), channel_id=1, source_target_pairs={{0,2},{2,4},{4,6},{6,8},{8,10},{10,12},{12,14},{14,0},{1,3},{3,5},... | collective-permute-start | bytes 786440 | tf_op jit(solution)/shard_map/ppermute | solution.py:17
  193.0 11.4 %collective-permute-start.29 = (bf16[64,2048]{1,0:T(8,128)(2,1)S(1)}, bf16[64,2048]{1,0:T(8,128)(2,1)S(1)}, u32[]{:S(2)}, u32[]{:S(2)}) collective-permute-start(bf16[64,2048]{1,0:T(8,128)(2,1)S(1)} %fusion.18), channel_id=1, source_target_pairs={{0,14},{2,0},{4,2},{6,4},{8,6},{10,8},{12,10},{14,12},{1,15},{3,1}... | collective-permute-start | bytes 786440 | tf_op jit(solution)/shard_map/ppermute | solution.py:17
  201.9 7.3 %collective-permute-start.20 = (bf16[64,2048]{1,0:T(8,128)(2,1)S(1)}, bf16[64,2048]{1,0:T(8,128)(2,1)S(1)}, u32[]{:S(2)}, u32[]{:S(2)}) collective-permute-start(bf16[64,2048]{1,0:T(8,128)(2,1)S(1)} %get-tuple-element.56), channel_id=1, source_target_pairs={{0,2},{2,4},{4,6},{6,8},{8,10},{10,12},{12,14},{14,0},{1,3},{3,5},... | collective-permute-start | bytes 786440 | tf_op jit(solution)/shard_map/ppermute | solution.py:17
  204.4 7.4 %collective-permute-start.23 = (bf16[64,2048]{1,0:T(8,128)(2,1)S(1)}, bf16[64,2048]{1,0:T(8,128)(2,1)S(1)}, u32[]{:S(2)}, u32[]{:S(2)}) collective-permute-start(bf16[64,2048]{1,0:T(8,128)(2,1)S(1)} %get-tuple-element.57), channel_id=1, source_target_pairs={{0,14},{2,0},{4,2},{6,4},{8,6},{10,8},{12,10},{14,12},{1,15},{3,1}... | collective-permute-start | bytes 786440 | tf_op jit(solution)/shard_map/ppermute | solution.py:17
  212.1 6.4 %collective-permute-start.26 = (bf16[64,2048]{1,0:T(8,128)(2,1)S(1)}, bf16[64,2048]{1,0:T(8,128)(2,1)S(1)}, u32[]{:S(2)}, u32[]{:S(2)}) collective-permute-start(bf16[64,2048]{1,0:T(8,128)(2,1)S(1)} %get-tuple-element.55), channel_id=1, source_target_pairs={{0,2},{2,4},{4,6},{6,8},{8,10},{10,12},{12,14},{14,0},{1,3},{3,5},... | collective-permute-start | bytes 786440 | tf_op jit(solution)/shard_map/ppermute | solution.py:17
  213.1 6.4 %collective-permute-start.30 = (bf16[64,2048]{1,0:T(8,128)(2,1)S(1)}, bf16[64,2048]{1,0:T(8,128)(2,1)S(1)}, u32[]{:S(2)}, u32[]{:S(2)}) collective-permute-start(bf16[64,2048]{1,0:T(8,128)(2,1)S(1)} %get-tuple-element.54), channel_id=1, source_target_pairs={{0,14},{2,0},{4,2},{6,4},{8,6},{10,8},{12,10},{14,12},{1,15},{3,1}... | collective-permute-start | bytes 786440 | tf_op jit(solution)/shard_map/ppermute | solution.py:17
where the time goes:
time: 225 us; the launch traced here: 221 us
  waiting for transfers between devices  91.4 us (41%)
  starting transfers between devices  75.6 us (34%)
  other arithmetic  13.9 us (6%)
  local copies, waits for them, and re-layouts  13.1 us (6%)
  Pallas kernels  13 us (6%)
  matrix products  12.8 us (6%)
    all_to_all x4, waiting for transfers between devices, plane_exchange(): lax.all_to_all(rows, ('y', 'x'), split_axis=0, concat_axis=0, tiled=True)  52.1 us
    ppermute x31, starting transfers between devices, shift(): lax.ppermute(block, axis, [(i, (i + by) % count) for i in range(count)])  43.3 us
    ppermute x31, waiting for transfers between devices, shift(): lax.ppermute(block, axis, [(i, (i + by) % count) for i in range(count)])  39.4 us
    all_to_all x4, starting transfers between devices, plane_exchange(): lax.all_to_all(rows, ('y', 'x'), split_axis=0, concat_axis=0, tiled=True)  32.4 us
    pallas_call x2, Pallas kernels, expert_rows(): pl.pallas_call(expert_kernel, grid=(count // block,), in_specs=[pl.BlockS...  13 us
    unnamed x26, local copies, waits for them, and re-layouts  9.85 us
    dot_general x8, matrix products, choose(): jnp.dot(one_hot, block_of(offset), preferred_element_type=jnp.float32)  9.66 us
    concatenate x2, other arithmetic, both_cores(): return jnp.concatenate([own, shift(own, 'c', CS, 1), last], axis=0)  5.14 us
  transfers between devices with their start and end apart: 35, of which 17 were waited for; matrix products, arithmetic and copies ran while one was open for 10% of the time, Pallas kernels for 2%

commit v1 on v0

--- a/solution.py
+++ b/solution.py
@@ -11,6 +11,7 @@
 NEAR = (0, -1, 1)
 FAR = (-2, 2, -3, 3, 4)
 ORDER = NEAR + FAR
+MEET = 2
 
 
 def shift(block, axis, count, by):
@@ -21,7 +22,7 @@
     return shift(block, "z", ZS, by)
 
 
-def ring_reduce(part):
+def ring_reduce(part, meet):
     far = ZS // 2
     lines = []
     for half in (0, 1):
@@ -29,6 +30,9 @@
             last = far if (half == 0) == (way == 1) else far - 1
             lines.append([half, way, last, None])
     for distance in range(far, 0, -1):
+        if distance == MEET:
+            for line, moving in zip(lines, meet([line[3] for line in lines])):
+                line[3] = moving
         for line in lines:
             half, way, last, moving = line
             if distance > last:
@@ -168,14 +172,19 @@
         mine = place == lax.broadcasted_iota(jnp.int32, (len(group) * tok_count, 1), 0)
         return jnp.dot(mine.astype(jnp.bfloat16), rows.reshape(-1, width), preferred_element_type=jnp.float32)
 
-    sums = {FAR: combine(FAR, far_back), NEAR: combine(NEAR, near_back)}
+    sums = {FAR: combine(FAR, far_back)}
+
+    def meet(moving):
+        moving, arrived = lax.optimization_barrier((moving, near_back))
+        sums[NEAR] = combine(NEAR, arrived)
+        return moving
 
     def part(offset, h):
         group = FAR if offset in FAR else NEAR
         start = group.index(offset) * tok_count + h * half
         return sums[group][start : start + half]
 
-    return ring_reduce(part)
+    return ring_reduce(part, meet)
 
 
 def solution(mesh):

time: 225 us -> 227 us (level)
  the two profiles are of different devices: /device:TPU:32 before, /device:TPU:2 now
where the time goes in v1:
time: 227 us; the launch traced here: 222 us
  starting transfers between devices  87.4 us (39%)
  waiting for transfers between devices  80.1 us (35%)
  matrix products  16.6 us (7%)
  Pallas kernels  13 us (6%)
  other arithmetic  12.4 us (5%)
  local copies, waits for them, and re-layouts  12.3 us (5%)
    ppermute x31, starting transfers between devices, shift(): lax.ppermute(block, axis, [(i, (i + by) % count) for i in range(count)])  48.6 us
    ppermute x31, waiting for transfers between devices, shift(): lax.ppermute(block, axis, [(i, (i + by) % count) for i in range(count)])  40.4 us
    all_to_all x4, waiting for transfers between devices, plane_exchange(): lax.all_to_all(rows, ('y', 'x'), split_axis=0, concat_axis=0, tiled=True)  39.7 us
    all_to_all x4, starting transfers between devices, plane_exchange(): lax.all_to_all(rows, ('y', 'x'), split_axis=0, concat_axis=0, tiled=True)  38.8 us
    pallas_call x2, Pallas kernels, expert_rows(): pl.pallas_call(expert_kernel, grid=(count // block,), in_specs=[pl.BlockS...  13 us
    unnamed x24, local copies, waits for them, and re-layouts  9.85 us
    dot_general x8, matrix products, choose(): jnp.dot(one_hot, block_of(offset), preferred_element_type=jnp.float32)  9.65 us
    dot_general x2, matrix products, combine(): jnp.dot(mine.astype(jnp.bfloat16), rows.reshape(-1, width), preferred_ele...  6.93 us
  transfers between devices with their start and end apart: 35, of which 20 were waited for; matrix products, arithmetic and copies ran while one was open for 12% of the time, Pallas kernels for 2%

profile of v1, /device:TPU:2, one launch (start us, length us, event | category | flops | bytes accessed | tf_op | source)
XLA Modules:
  0.0 222.3 jit_solution(9688433766642130085)
XLA Ops:
  4.0 2.0 collective-permute-start
  6.0 4.0 %collective-permute-start.3 = (bf16[72,2048]{1,0:T(8,128)(2,1)S(1)}, bf16[72,2048]{1,0:T(8,128)(2,1)S(1)}, u32[]{:S(2)}, u32[]{:S(2)}) collective-permute-start(bf16[72,2048]{1,0:T(8,128)(2,1)S(1)} %fusion.52), channel_id=1, source_target_pairs={{0,14},{2,0},{4,2},{6,4},{8,6},{10,8},{12,10},{14,12},{1,15},{3,1}... | collective-permute-start | bytes 884744 | tf_op jit(solution)/shard_map/ppermute | solution.py:18
  10.0 3.2 %collective-permute-start.8 = (bf16[64,2048]{1,0:T(8,128)(2,1)S(1)}, bf16[64,2048]{1,0:T(8,128)(2,1)S(1)}, u32[]{:S(2)}, u32[]{:S(2)}) collective-permute-start(bf16[64,2048]{1,0:T(8,128)(2,1)S(1)} %get-tuple-element.75), channel_id=1, source_target_pairs={{0,14},{2,0},{4,2},{6,4},{8,6},{10,8},{12,10},{14,12},{1,15},{3,1}... | collective-permute-start | bytes 786440 | tf_op jit(solution)/shard_map/ppermute | solution.py:18
  13.3 1.4 fusion
  14.6 7.9 %collective-permute-done.7 = bf16[64,2048]{1,0:T(8,128)(2,1)S(1)} collective-permute-done((bf16[64,2048]{1,0:T(8,128)(2,1)S(1)}, bf16[64,2048]{1,0:T(8,128)(2,1)S(1)}, u32[]{:S(2)}, u32[]{:S(2)}) %collective-permute-start.7) | collective-permute-done | bytes 262176 | tf_op jit(solution)/shard_map/ppermute | solution.py:18
  22.6 3.2 %collective-permute-start.10 = (bf16[64,2048]{1,0:T(8,128)(2,1)S(1)}, bf16[64,2048]{1,0:T(8,128)(2,1)}, u32[]{:S(2)}, u32[]{:S(2)}) collective-permute-start(bf16[64,2048]{1,0:T(8,128)(2,1)S(1)} %collective-permute-done.8), channel_id=1, source_target_pairs={{0,14},{2,0},{4,2},{6,4},{8,6},{10,8},{12,10},{14,12},{1,15},{3,1}... | collective-permute-start | bytes 786440 | tf_op jit(solution)/shard_map/ppermute | solution.py:18
  25.8 3.2 %collective-permute-start.4 = (bf16[72,2048]{1,0:T(8,128)(2,1)S(1)}, bf16[72,2048]{1,0:T(8,128)(2,1)S(1)}, u32[]{:S(2)}, u32[]{:S(2)}) collective-permute-start(bf16[72,2048]{1,0:T(8,128)(2,1)S(1)} %collective-permute-done.3), channel_id=1, source_target_pairs={{0,14},{2,0},{4,2},{6,4},{8,6},{10,8},{12,10},{14,12},{1,15},{3,1}... | collective-permute-start | bytes 884744 | tf_op jit(solution)/shard_map/ppermute | solution.py:18
  31.1 7.5 %all-to-all-start = ((bf16[16,24,2048]{2,1,0:T(8,128)(2,1)}), bf16[16,24,2048]{2,1,0:T(8,128)(2,1)S(1)}, u32[]{:S(2)}, u32[]{:S(2)}) async-start(bf16[16,24,2048]{2,1,0:T(8,128)(2,1)} %pad_maximum_fusion.1), calls=%async_computation | async-start | bytes 3145728 | tf_op jit(solution)/shard_map/all_to_all | solution.py:55
  38.7 3.2 %collective-permute-start.12 = (bf16[64,2048]{1,0:T(8,128)(2,1)}, bf16[64,2048]{1,0:T(8,128)(2,1)S(1)}, u32[]{:S(2)}, u32[]{:S(2)}) collective-permute-start(bf16[64,2048]{1,0:T(8,128)(2,1)} %collective-permute-done.10), channel_id=1, source_target_pairs={{0,14},{2,0},{4,2},{6,4},{8,6},{10,8},{12,10},{14,12},{1,15},{3,1}... | collective-permute-start | bytes 786440 | tf_op jit(solution)/shard_map/ppermute | solution.py:18
  42.0 3.3 %collective-permute-start.5 = (bf16[72,2048]{1,0:T(8,128)(2,1)S(1)}, bf16[72,2048]{1,0:T(8,128)(2,1)S(1)}, u32[]{:S(2)}, u32[]{:S(2)}) collective-permute-start(bf16[72,2048]{1,0:T(8,128)(2,1)S(1)} %collective-permute-done.4), channel_id=1, source_target_pairs={{0,14},{2,0},{4,2},{6,4},{8,6},{10,8},{12,10},{14,12},{1,15},{3,1}... | collective-permute-start | bytes 884744 | tf_op jit(solution)/shard_map/ppermute | solution.py:18
  45.3 2.1 fusion.4
  47.4 2.1 fusion.6
  49.5 3.1 %collective-permute-start.13 = (bf16[64,2048]{1,0:T(8,128)(2,1)S(1)}, bf16[64,2048]{1,0:T(8,128)(2,1)S(1)}, u32[]{:S(2)}, u32[]{:S(2)}) collective-permute-start(bf16[64,2048]{1,0:T(8,128)(2,1)S(1)} %collective-permute-done.12), channel_id=1, source_target_pairs={{0,14},{2,0},{4,2},{6,4},{8,6},{10,8},{12,10},{14,12},{1,15},{3,1}... | collective-permute-start | bytes 786440 | tf_op jit(solution)/shard_map/ppermute | solution.py:18
  52.9 1.4 collective-permute-done.5
  56.6 4.1 %collective-permute-done.6 = bf16[72,2048]{1,0:T(8,128)(2,1)S(1)} collective-permute-done((bf16[72,2048]{1,0:T(8,128)(2,1)S(1)}, bf16[72,2048]{1,0:T(8,128)(2,1)S(1)}, u32[]{:S(2)}, u32[]{:S(2)}) %collective-permute-start.6) | collective-permute-done | bytes 294944 | tf_op jit(solution)/shard_map/ppermute | solution.py:18
  61.9 7.5 %all-to-all-start.1 = ((bf16[16,40,2048]{2,1,0:T(8,128)(2,1)}), bf16[16,40,2048]{2,1,0:T(8,128)(2,1)}, u32[]{:S(2)}, u32[]{:S(2)}) async-start(bf16[16,40,2048]{2,1,0:T(8,128)(2,1)} %fusion.12), calls=%async_computation.1 | async-start | bytes 5242880 | tf_op jit(solution)/shard_map/all_to_all | solution.py:55
  70.2 3.7 %collective-permute-done.14 = bf16[352,2048]{1,0:T(8,128)(2,1)} collective-permute-done((bf16[352,2048]{1,0:T(8,128)(2,1)S(1)}, bf16[352,2048]{1,0:T(8,128)(2,1)}, u32[]{:S(2)}, u32[]{:S(2)}) %collective-permute-start.14) | collective-permute-done | bytes 1441824 | tf_op jit(solution)/shard_map/ppermute | solution.py:18
  74.0 1.9 pad_maximum_fusion.gate_ref
  77.2 3.2 %maximum_maximum_fusion.1 = (bf16[768,2048]{1,0:T(8,128)(2,1)S(1)}, bf16[768,2048]{1,0:T(8,128)(2,1)S(1)}) fusion(bf16[352,2048]{1,0:T(8,128)(2,1)} %collective-permute-done.16, bf16[352,2048]{1,0:T(8,128)(2,1)} %bitcast.34, bf16[768]{0:T(1024)(128)(2,1)S(1)} %pad.12.clone, bf16[352,2048]{1,0:T(8,128)(2,1)} %collective-permute-done.15, ...), kind=kLoop, calls=%fused_computation.2 | loop fusion | flops 17301504 | bytes 12060160 | tf_op jit(solution)/shard_map/concatenate | solution.py:128
  80.5 5.1 %shard_map.73 = bf16[384,2048]{1,0:T(8,128)(2,1)} custom-call(s32[1]{0:T(128)} %bitcast.10.column_ref, bf16[384,2048]{1,0:T(8,128)(2,1)S(1)} %bitcast.93, bf16[768,2048]{1,0:T(8,128)(2,1)S(1)} %pad_maximum_fusion.gate_ref, bf16[768,2048]{1,0:T(8,128)(2,1)S(1)} %get-tuple-element.77.up_ref, bf16[768,2048]{1,0:T(8,128)(2,1)S(1)} %get-tuple-element.76.down_ref), custom_call_target="tpu_custom_call" | custom-call | tf_op jit(solution)/shard_map/pallas_call | solution.py:75
  85.5 1.7 copy-done
  87.2 1.6 copy-done.2
  88.8 10.6 %all-to-all-done.1 = bf16[16,40,2048]{2,1,0:T(8,128)(2,1)} async-done(((bf16[16,40,2048]{2,1,0:T(8,128)(2,1)}), bf16[16,40,2048]{2,1,0:T(8,128)(2,1)}, u32[]{:S(2)}, u32[]{:S(2)}) %all-to-all-start.1) | async-done | bytes 2621472 | tf_op jit(solution)/shard_map/all_to_all | solution.py:55
  99.4 1.9 copy-done.1
  101.3 1.9 copy-done.3
  103.2 7.9 %shard_map.74 = bf16[640,2048]{1,0:T(8,128)(2,1)S(1)} custom-call(s32[1]{0:T(128)} %bitcast.10.column_ref, bf16[640,2048]{1,0:T(8,128)(2,1)} %bitcast.36.rows_ref, bf16[768,2048]{1,0:T(8,128)(2,1)S(1)} %pad_maximum_fusion.gate_ref, bf16[768,2048]{1,0:T(8,128)(2,1)S(1)} %copy-done.3, bf16[768,2048]{1,0:T(8,128)(2,1)S(1)} %copy-done.1), custom_call_target="tpu_custom_call" | custom-call | tf_op jit(solution)/shard_map/pallas_call | solution.py:75
  111.1 1.5 copy-done.4
  112.5 6.3 %all-to-all-start.2 = ((bf16[16,40,2048]{2,1,0:T(8,128)(2,1)}), bf16[16,40,2048]{2,1,0:T(8,128)(2,1)S(1)}, u32[]{:S(2)}, u32[]{:S(2)}) async-start(bf16[16,40,2048]{2,1,0:T(8,128)(2,1)} %bitcast.92), calls=%async_computation.2 | async-start | bytes 5242880 | tf_op jit(solution)/shard_map/all_to_all | solution.py:55
  119.4 29.2 %all-to-all-done.2 = bf16[16,40,2048]{2,1,0:T(8,128)(2,1)S(1)} async-done(((bf16[16,40,2048]{2,1,0:T(8,128)(2,1)}), bf16[16,40,2048]{2,1,0:T(8,128)(2,1)S(1)}, u32[]{:S(2)}, u32[]{:S(2)}) %all-to-all-start.2) | async-done | bytes 2621472 | tf_op jit(solution)/shard_map/all_to_all | solution.py:55
  148.6 17.5 %all-to-all-start.3 = ((bf16[16,24,2048]{2,1,0:T(8,128)(2,1)}), bf16[16,24,2048]{2,1,0:T(8,128)(2,1)}, u32[]{:S(2)}, u32[]{:S(2)}) async-start(bf16[16,24,2048]{2,1,0:T(8,128)(2,1)} %bitcast.35), calls=%async_computation.3 | async-start | bytes 3145728 | tf_op jit(solution)/shard_map/all_to_all | solution.py:55
  166.1 4.5 %fusion.111 = (bf16[640,2048]{1,0:T(8,128)(2,1)S(1)}, f32[640,2048]{1,0:T(8,128)}) fusion(bf16[640,2048]{1,0:T(8,128)(2,1)S(1)} %bitcast.94, s32[640]{0:T(1024)S(1)} %fusion.65), kind=kOutput, calls=%fused_computation.173 | convolution fusion | flops 1679441920 | bytes 10488320 | tf_op jit(solution)/shard_map/dot_general | solution.py:173
  170.8 1.4 collective-permute-start.17
  172.2 2.0 collective-permute-start.21
  174.4 2.0 collective-permute-start.19
  176.5 3.3 %collective-permute-done.17 = bf16[64,2048]{1,0:T(8,128)(2,1)S(1)} collective-permute-done((bf16[64,2048]{1,0:T(8,128)(2,1)S(1)}, bf16[64,2048]{1,0:T(8,128)(2,1)S(1)}, u32[]{:S(2)}, u32[]{:S(2)}) %collective-permute-start.17) | collective-permute-done | bytes 262176 | tf_op jit(solution)/shard_map/ppermute | solution.py:18
  182.5 2.0 collective-permute-start.18
  184.5 1.6 collective-permute-start.22
  186.9 3.5 %collective-permute-done.18 = bf16[64,2048]{1,0:T(8,128)(2,1)S(1)} collective-permute-done((bf16[64,2048]{1,0:T(8,128)(2,1)S(1)}, bf16[64,2048]{1,0:T(8,128)(2,1)S(1)}, u32[]{:S(2)}, u32[]{:S(2)}) %collective-permute-start.18) | collective-permute-done | bytes 262176 | tf_op jit(solution)/shard_map/ppermute | solution.py:18
  190.9 1.8 fusion.25
  192.7 1.9 collective-permute-start.23
  194.6 1.4 collective-permute-start.25
  196.7 2.6 %collective-permute-start.29 = (bf16[64,2048]{1,0:T(8,128)(2,1)S(1)}, bf16[64,2048]{1,0:T(8,128)(2,1)S(1)}, u32[]{:S(2)}, u32[]{:S(2)}) collective-permute-start(bf16[64,2048]{1,0:T(8,128)(2,1)S(1)} %get-tuple-element.60), channel_id=1, source_target_pairs={{0,14},{2,0},{4,2},{6,4},{8,6},{10,8},{12,10},{14,12},{1,15},{3,1}... | collective-permute-start | bytes 786440 | tf_op jit(solution)/shard_map/ppermute | solution.py:18
  199.3 2.4 %fusion.15 = f32[384,2048]{1,0:T(8,128)S(1)} fusion(bf16[384,2048]{1,0:T(8,128)(2,1)} %bitcast.39, s32[384]{0:T(512)S(1)} %fusion.75), kind=kOutput, calls=%fused_computation.30 | convolution fusion | flops 604127232 | bytes 4720128 | tf_op jit(solution)/shard_map/dot_general | solution.py:173
  203.2 2.1 collective-permute-start.24
  207.2 3.6 %collective-permute-done.24 = bf16[64,2048]{1,0:T(8,128)(2,1)S(1)} collective-permute-done((bf16[64,2048]{1,0:T(8,128)(2,1)S(1)}, bf16[64,2048]{1,0:T(8,128)(2,1)S(1)}, u32[]{:S(2)}, u32[]{:S(2)}) %collective-permute-start.24) | collective-permute-done | bytes 262176 | tf_op jit(solution)/shard_map/ppermute | solution.py:18
  210.9 2.4 %collective-permute-done.26 = bf16[64,2048]{1,0:T(8,128)(2,1)S(1)} collective-permute-done((bf16[64,2048]{1,0:T(8,128)(2,1)S(1)}, bf16[64,2048]{1,0:T(8,128)(2,1)S(1)}, u32[]{:S(2)}, u32[]{:S(2)}) %collective-permute-start.26) | collective-permute-done | bytes 262176 | tf_op jit(solution)/shard_map/ppermute | solution.py:18
  213.7 3.1 %collective-permute-start.30 = (bf16[64,2048]{1,0:T(8,128)(2,1)S(1)}, bf16[64,2048]{1,0:T(8,128)(2,1)S(1)}, u32[]{:S(2)}, u32[]{:S(2)}) collective-permute-start(bf16[64,2048]{1,0:T(8,128)(2,1)S(1)} %get-tuple-element.66), channel_id=1, source_target_pairs={{0,14},{2,0},{4,2},{6,4},{8,6},{10,8},{12,10},{14,12},{1,15},{3,1}... | collective-permute-start | bytes 786440 | tf_op jit(solution)/shard_map/ppermute | solution.py:18
  216.8 4.3 %collective-permute-done.28 = bf16[64,2048]{1,0:T(8,128)(2,1)S(1)} collective-permute-done((bf16[64,2048]{1,0:T(8,128)(2,1)S(1)}, bf16[64,2048]{1,0:T(8,128)(2,1)S(1)}, u32[]{:S(2)}, u32[]{:S(2)}) %collective-permute-start.28) | collective-permute-done | bytes 262176 | tf_op jit(solution)/shard_map/ppermute | solution.py:18
  (109 shorter events, 22.4 us)
Async XLA Ops:
  4.0 21.8 %collective-permute-start = (bf16[72,2048]{1,0:T(8,128)(2,1)S(1)}, bf16[72,2048]{1,0:T(8,128)(2,1)S(1)}, u32[]{:S(2)}, u32[]{:S(2)}) collective-permute-start(bf16[72,2048]{1,0:T(8,128)(2,1)S(1)} %fusion.52), channel_id=1, source_target_pairs={{0,2},{2,4},{4,6},{6,8},{8,10},{10,12},{12,14},{14,0},{1,3},{3,5},... | collective-permute-start | bytes 884744 | tf_op jit(solution)/shard_map/ppermute | solution.py:18
  6.0 19.8 %collective-permute-start.3 = (bf16[72,2048]{1,0:T(8,128)(2,1)S(1)}, bf16[72,2048]{1,0:T(8,128)(2,1)S(1)}, u32[]{:S(2)}, u32[]{:S(2)}) collective-permute-start(bf16[72,2048]{1,0:T(8,128)(2,1)S(1)} %fusion.52), channel_id=1, source_target_pairs={{0,14},{2,0},{4,2},{6,4},{8,6},{10,8},{12,10},{14,12},{1,15},{3,1}... | collective-permute-start | bytes 884744 | tf_op jit(solution)/shard_map/ppermute | solution.py:18
  10.0 12.5 %collective-permute-start.7 = (bf16[64,2048]{1,0:T(8,128)(2,1)S(1)}, bf16[64,2048]{1,0:T(8,128)(2,1)S(1)}, u32[]{:S(2)}, u32[]{:S(2)}) collective-permute-start(bf16[64,2048]{1,0:T(8,128)(2,1)S(1)} %get-tuple-element.75), channel_id=1, source_target_pairs={{0,2},{2,4},{4,6},{6,8},{8,10},{10,12},{12,14},{14,0},{1,3},{3,5},... | collective-permute-start | bytes 786440 | tf_op jit(solution)/shard_map/ppermute | solution.py:18
  10.0 12.5 %collective-permute-start.8 = (bf16[64,2048]{1,0:T(8,128)(2,1)S(1)}, bf16[64,2048]{1,0:T(8,128)(2,1)S(1)}, u32[]{:S(2)}, u32[]{:S(2)}) collective-permute-start(bf16[64,2048]{1,0:T(8,128)(2,1)S(1)} %get-tuple-element.75), channel_id=1, source_target_pairs={{0,14},{2,0},{4,2},{6,4},{8,6},{10,8},{12,10},{14,12},{1,15},{3,1}... | collective-permute-start | bytes 786440 | tf_op jit(solution)/shard_map/ppermute | solution.py:18
  22.6 16.0 %collective-permute-start.9 = (bf16[64,2048]{1,0:T(8,128)(2,1)S(1)}, bf16[64,2048]{1,0:T(8,128)(2,1)}, u32[]{:S(2)}, u32[]{:S(2)}) collective-permute-start(bf16[64,2048]{1,0:T(8,128)(2,1)S(1)} %collective-permute-done.7), channel_id=1, source_target_pairs={{0,2},{2,4},{4,6},{6,8},{8,10},{10,12},{12,14},{14,0},{1,3},{3,5},... | collective-permute-start | bytes 786440 | tf_op jit(solution)/shard_map/ppermute | solution.py:18
  22.6 16.1 %collective-permute-start.10 = (bf16[64,2048]{1,0:T(8,128)(2,1)S(1)}, bf16[64,2048]{1,0:T(8,128)(2,1)}, u32[]{:S(2)}, u32[]{:S(2)}) collective-permute-start(bf16[64,2048]{1,0:T(8,128)(2,1)S(1)} %collective-permute-done.8), channel_id=1, source_target_pairs={{0,14},{2,0},{4,2},{6,4},{8,6},{10,8},{12,10},{14,12},{1,15},{3,1}... | collective-permute-start | bytes 786440 | tf_op jit(solution)/shard_map/ppermute | solution.py:18
  25.8 16.1 %collective-permute-start.1 = (bf16[72,2048]{1,0:T(8,128)(2,1)S(1)}, bf16[72,2048]{1,0:T(8,128)(2,1)S(1)}, u32[]{:S(2)}, u32[]{:S(2)}) collective-permute-start(bf16[72,2048]{1,0:T(8,128)(2,1)S(1)} %collective-permute-done), channel_id=1, source_target_pairs={{0,2},{2,4},{4,6},{6,8},{8,10},{10,12},{12,14},{14,0},{1,3},{3,5},... | collective-permute-start | bytes 884744 | tf_op jit(solution)/shard_map/ppermute | solution.py:18
  25.8 16.1 %collective-permute-start.4 = (bf16[72,2048]{1,0:T(8,128)(2,1)S(1)}, bf16[72,2048]{1,0:T(8,128)(2,1)S(1)}, u32[]{:S(2)}, u32[]{:S(2)}) collective-permute-start(bf16[72,2048]{1,0:T(8,128)(2,1)S(1)} %collective-permute-done.3), channel_id=1, source_target_pairs={{0,14},{2,0},{4,2},{6,4},{8,6},{10,8},{12,10},{14,12},{1,15},{3,1}... | collective-permute-start | bytes 884744 | tf_op jit(solution)/shard_map/ppermute | solution.py:18
  31.1 30.8 %all-to-all-start = ((bf16[16,24,2048]{2,1,0:T(8,128)(2,1)}), bf16[16,24,2048]{2,1,0:T(8,128)(2,1)S(1)}, u32[]{:S(2)}, u32[]{:S(2)}) async-start(bf16[16,24,2048]{2,1,0:T(8,128)(2,1)} %pad_maximum_fusion.1), calls=%async_computation | async-start | bytes 3145728 | tf_op jit(solution)/shard_map/all_to_all | solution.py:55
  38.6 15.8 %collective-permute-start.11 = (bf16[64,2048]{1,0:T(8,128)(2,1)}, bf16[64,2048]{1,0:T(8,128)(2,1)S(1)}, u32[]{:S(2)}, u32[]{:S(2)}) collective-permute-start(bf16[64,2048]{1,0:T(8,128)(2,1)} %collective-permute-done.9), channel_id=1, source_target_pairs={{0,2},{2,4},{4,6},{6,8},{8,10},{10,12},{12,14},{14,0},{1,3},{3,5},... | collective-permute-start | bytes 786440 | tf_op jit(solution)/shard_map/ppermute | solution.py:18
  38.7 10.8 %collective-permute-start.12 = (bf16[64,2048]{1,0:T(8,128)(2,1)}, bf16[64,2048]{1,0:T(8,128)(2,1)S(1)}, u32[]{:S(2)}, u32[]{:S(2)}) collective-permute-start(bf16[64,2048]{1,0:T(8,128)(2,1)} %collective-permute-done.10), channel_id=1, source_target_pairs={{0,14},{2,0},{4,2},{6,4},{8,6},{10,8},{12,10},{14,12},{1,15},{3,1}... | collective-permute-start | bytes 786440 | tf_op jit(solution)/shard_map/ppermute | solution.py:18
  41.9 10.7 %collective-permute-start.2 = (bf16[72,2048]{1,0:T(8,128)(2,1)S(1)}, bf16[72,2048]{1,0:T(8,128)(2,1)S(1)}, u32[]{:S(2)}, u32[]{:S(2)}) collective-permute-start(bf16[72,2048]{1,0:T(8,128)(2,1)S(1)} %collective-permute-done.1), channel_id=1, source_target_pairs={{0,2},{2,4},{4,6},{6,8},{8,10},{10,12},{12,14},{14,0},{1,3},{3,5},... | collective-permute-start | bytes 884744 | tf_op jit(solution)/shard_map/ppermute | solution.py:18
  42.0 12.3 %collective-permute-start.5 = (bf16[72,2048]{1,0:T(8,128)(2,1)S(1)}, bf16[72,2048]{1,0:T(8,128)(2,1)S(1)}, u32[]{:S(2)}, u32[]{:S(2)}) collective-permute-start(bf16[72,2048]{1,0:T(8,128)(2,1)S(1)} %collective-permute-done.4), channel_id=1, source_target_pairs={{0,14},{2,0},{4,2},{6,4},{8,6},{10,8},{12,10},{14,12},{1,15},{3,1}... | collective-permute-start | bytes 884744 | tf_op jit(solution)/shard_map/ppermute | solution.py:18
  49.5 11.3 %collective-permute-start.13 = (bf16[64,2048]{1,0:T(8,128)(2,1)S(1)}, bf16[64,2048]{1,0:T(8,128)(2,1)S(1)}, u32[]{:S(2)}, u32[]{:S(2)}) collective-permute-start(bf16[64,2048]{1,0:T(8,128)(2,1)S(1)} %collective-permute-done.12), channel_id=1, source_target_pairs={{0,14},{2,0},{4,2},{6,4},{8,6},{10,8},{12,10},{14,12},{1,15},{3,1}... | collective-permute-start | bytes 786440 | tf_op jit(solution)/shard_map/ppermute | solution.py:18
  52.6 8.2 %collective-permute-start.6 = (bf16[72,2048]{1,0:T(8,128)(2,1)S(1)}, bf16[72,2048]{1,0:T(8,128)(2,1)S(1)}, u32[]{:S(2)}, u32[]{:S(2)}) collective-permute-start(bf16[72,2048]{1,0:T(8,128)(2,1)S(1)} %collective-permute-done.2), channel_id=1, source_target_pairs={{0,2},{2,4},{4,6},{6,8},{8,10},{10,12},{12,14},{14,0},{1,3},{3,5},... | collective-permute-start | bytes 884744 | tf_op jit(solution)/shard_map/ppermute | solution.py:18
  61.9 7.5 %copy-start.7 = (bf16[1,2048,352]{1,2,0:T(8,128)(2,1)S(1)}, bf16[1,2048,352]{1,2,0:T(8,128)(2,1)}, u32[]{:S(2)}) copy-start(bf16[1,2048,352]{1,2,0:T(8,128)(2,1)} %param.9) | copy-start | bytes 4325380
  61.9 12.0 %copy-start.8 = (bf16[2048,64]{0,1:T(8,128)(2,1)S(1)}, bf16[2048,64]{0,1:T(8,128)(2,1)}, u32[]{:S(2)}) copy-start(bf16[2048,64]{0,1:T(8,128)(2,1)} %param.8) | copy-start | bytes 786436
  61.9 7.5 %copy-start.5 = (bf16[16,24,2048]{2,1,0:T(8,128)(2,1)}, bf16[16,24,2048]{2,1,0:T(8,128)(2,1)S(1)}, u32[]{:S(2)}) copy-start(bf16[16,24,2048]{2,1,0:T(8,128)(2,1)S(1)} %all-to-all-done) | copy-start | bytes 4718596
  61.9 37.4 %all-to-all-start.1 = ((bf16[16,40,2048]{2,1,0:T(8,128)(2,1)}), bf16[16,40,2048]{2,1,0:T(8,128)(2,1)}, u32[]{:S(2)}, u32[]{:S(2)}) async-start(bf16[16,40,2048]{2,1,0:T(8,128)(2,1)} %fusion.12), calls=%async_computation.1 | async-start | bytes 5242880 | tf_op jit(solution)/shard_map/all_to_all | solution.py:55
  69.5 4.5 %collective-permute-start.14 = (bf16[352,2048]{1,0:T(8,128)(2,1)S(1)}, bf16[352,2048]{1,0:T(8,128)(2,1)}, u32[]{:S(2)}, u32[]{:S(2)}) collective-permute-start(bf16[352,2048]{1,0:T(8,128)(2,1)S(1)} %bitcast.96), channel_id=1, source_target_pairs={{0,1},{1,0},{2,3},{3,2},{4,5},{5,4},{6,7},{7,6},{8,9},{9,8},{10,11... | collective-permute-start | bytes 4325384 | tf_op jit(solution)/shard_map/ppermute | solution.py:18
  69.6 6.4 %collective-permute-start.15 = (bf16[352,2048]{1,0:T(8,128)(2,1)}, bf16[352,2048]{1,0:T(8,128)(2,1)}, u32[]{:S(2)}, u32[]{:S(2)}) collective-permute-start(bf16[352,2048]{1,0:T(8,128)(2,1)} %bitcast.32), channel_id=1, source_target_pairs={{0,1},{1,0},{2,3},{3,2},{4,5},{5,4},{6,7},{7,6},{8,9},{9,8},{10,11... | collective-permute-start | bytes 4325384 | tf_op jit(solution)/shard_map/ppermute | solution.py:18
  70.1 7.2 %collective-permute-start.16 = (bf16[352,2048]{1,0:T(8,128)(2,1)}, bf16[352,2048]{1,0:T(8,128)(2,1)}, u32[]{:S(2)}, u32[]{:S(2)}) collective-permute-start(bf16[352,2048]{1,0:T(8,128)(2,1)} %bitcast.34), channel_id=1, source_target_pairs={{0,1},{1,0},{2,3},{3,2},{4,5},{5,4},{6,7},{7,6},{8,9},{9,8},{10,11... | collective-permute-start | bytes 4325384 | tf_op jit(solution)/shard_map/ppermute | solution.py:18
  75.9 4.5 %copy-start.6 = (bf16[16,24,2048]{2,1,0:T(8,128)(2,1)S(1)}, bf16[16,24,2048]{2,1,0:T(8,128)(2,1)}, u32[]{:S(2)}) copy-start(bf16[16,24,2048]{2,1,0:T(8,128)(2,1)} %copy-done.5) | copy-start | bytes 4718596
  85.5 1.7 copy-start
  87.2 1.6 copy-start.2
  99.4 1.9 copy-start.1
  101.3 1.9 copy-start.3
  111.1 1.5 copy-start.4
  112.5 36.1 %all-to-all-start.2 = ((bf16[16,40,2048]{2,1,0:T(8,128)(2,1)}), bf16[16,40,2048]{2,1,0:T(8,128)(2,1)S(1)}, u32[]{:S(2)}, u32[]{:S(2)}) async-start(bf16[16,40,2048]{2,1,0:T(8,128)(2,1)} %bitcast.92), calls=%async_computation.2 | async-start | bytes 5242880 | tf_op jit(solution)/shard_map/all_to_all | solution.py:55
  148.6 42.3 %all-to-all-start.3 = ((bf16[16,24,2048]{2,1,0:T(8,128)(2,1)}), bf16[16,24,2048]{2,1,0:T(8,128)(2,1)}, u32[]{:S(2)}, u32[]{:S(2)}) async-start(bf16[16,24,2048]{2,1,0:T(8,128)(2,1)} %bitcast.35), calls=%async_computation.3 | async-start | bytes 3145728 | tf_op jit(solution)/shard_map/all_to_all | solution.py:55
  170.8 9.1 %collective-permute-start.17 = (bf16[64,2048]{1,0:T(8,128)(2,1)S(1)}, bf16[64,2048]{1,0:T(8,128)(2,1)S(1)}, u32[]{:S(2)}, u32[]{:S(2)}) collective-permute-start(bf16[64,2048]{1,0:T(8,128)(2,1)S(1)} %get-tuple-element.73), channel_id=1, source_target_pairs={{0,2},{2,4},{4,6},{6,8},{8,10},{10,12},{12,14},{14,0},{1,3},{3,5},... | collective-permute-start | bytes 786440 | tf_op jit(solution)/shard_map/ppermute | solution.py:18
  172.2 9.1 %collective-permute-start.21 = (bf16[64,2048]{1,0:T(8,128)(2,1)S(1)}, bf16[64,2048]{1,0:T(8,128)(2,1)S(1)}, u32[]{:S(2)}, u32[]{:S(2)}) collective-permute-start(bf16[64,2048]{1,0:T(8,128)(2,1)S(1)} %get-tuple-element.70), channel_id=1, source_target_pairs={{0,14},{2,0},{4,2},{6,4},{8,6},{10,8},{12,10},{14,12},{1,15},{3,1}... | collective-permute-start | bytes 786440 | tf_op jit(solution)/shard_map/ppermute | solution.py:18
  174.4 12.1 %collective-permute-start.19 = (bf16[64,2048]{1,0:T(8,128)(2,1)S(1)}, bf16[64,2048]{1,0:T(8,128)(2,1)S(1)}, u32[]{:S(2)}, u32[]{:S(2)}) collective-permute-start(bf16[64,2048]{1,0:T(8,128)(2,1)S(1)} %get-tuple-element.72), channel_id=1, source_target_pairs={{0,14},{2,0},{4,2},{6,4},{8,6},{10,8},{12,10},{14,12},{1,15},{3,1}... | collective-permute-start | bytes 786440 | tf_op jit(solution)/shard_map/ppermute | solution.py:18
  176.4 10.5 %collective-permute-start.20 = (bf16[64,2048]{1,0:T(8,128)(2,1)S(1)}, bf16[64,2048]{1,0:T(8,128)(2,1)S(1)}, u32[]{:S(2)}, u32[]{:S(2)}) collective-permute-start(bf16[64,2048]{1,0:T(8,128)(2,1)S(1)} %get-tuple-element.71), channel_id=1, source_target_pairs={{0,2},{2,4},{4,6},{6,8},{8,10},{10,12},{12,14},{14,0},{1,3},{3,5},... | collective-permute-start | bytes 786440 | tf_op jit(solution)/shard_map/ppermute | solution.py:18
  182.5 7.8 %collective-permute-start.18 = (bf16[64,2048]{1,0:T(8,128)(2,1)S(1)}, bf16[64,2048]{1,0:T(8,128)(2,1)S(1)}, u32[]{:S(2)}, u32[]{:S(2)}) collective-permute-start(bf16[64,2048]{1,0:T(8,128)(2,1)S(1)} %get-tuple-element.64), channel_id=1, source_target_pairs={{0,2},{2,4},{4,6},{6,8},{8,10},{10,12},{12,14},{14,0},{1,3},{3,5},... | collective-permute-start | bytes 786440 | tf_op jit(solution)/shard_map/ppermute | solution.py:18
  184.5 6.4 %collective-permute-start.22 = (bf16[64,2048]{1,0:T(8,128)(2,1)S(1)}, bf16[64,2048]{1,0:T(8,128)(2,1)S(1)}, u32[]{:S(2)}, u32[]{:S(2)}) collective-permute-start(bf16[64,2048]{1,0:T(8,128)(2,1)S(1)} %get-tuple-element.63), channel_id=1, source_target_pairs={{0,14},{2,0},{4,2},{6,4},{8,6},{10,8},{12,10},{14,12},{1,15},{3,1}... | collective-permute-start | bytes 786440 | tf_op jit(solution)/shard_map/ppermute | solution.py:18
  192.7 9.1 %collective-permute-start.23 = (bf16[64,2048]{1,0:T(8,128)(2,1)S(1)}, bf16[64,2048]{1,0:T(8,128)(2,1)S(1)}, u32[]{:S(2)}, u32[]{:S(2)}) collective-permute-start(bf16[64,2048]{1,0:T(8,128)(2,1)S(1)} %get-tuple-element.59), channel_id=1, source_target_pairs={{0,2},{2,4},{4,6},{6,8},{8,10},{10,12},{12,14},{14,0},{1,3},{3,5},... | collective-permute-start | bytes 786440 | tf_op jit(solution)/shard_map/ppermute | solution.py:18
  194.6 8.4 %collective-permute-start.25 = (bf16[64,2048]{1,0:T(8,128)(2,1)S(1)}, bf16[64,2048]{1,0:T(8,128)(2,1)S(1)}, u32[]{:S(2)}, u32[]{:S(2)}) collective-permute-start(bf16[64,2048]{1,0:T(8,128)(2,1)S(1)} %get-tuple-element.62), channel_id=1, source_target_pairs={{0,14},{2,0},{4,2},{6,4},{8,6},{10,8},{12,10},{14,12},{1,15},{3,1}... | collective-permute-start | bytes 786440 | tf_op jit(solution)/shard_map/ppermute | solution.py:18
  196.0 11.1 %collective-permute-start.27 = (bf16[64,2048]{1,0:T(8,128)(2,1)S(1)}, bf16[64,2048]{1,0:T(8,128)(2,1)S(1)}, u32[]{:S(2)}, u32[]{:S(2)}) collective-permute-start(bf16[64,2048]{1,0:T(8,128)(2,1)S(1)} %get-tuple-element.61), channel_id=1, source_target_pairs={{0,2},{2,4},{4,6},{6,8},{8,10},{10,12},{12,14},{14,0},{1,3},{3,5},... | collective-permute-start | bytes 786440 | tf_op jit(solution)/shard_map/ppermute | solution.py:18
  196.7 10.6 %collective-permute-start.29 = (bf16[64,2048]{1,0:T(8,128)(2,1)S(1)}, bf16[64,2048]{1,0:T(8,128)(2,1)S(1)}, u32[]{:S(2)}, u32[]{:S(2)}) collective-permute-start(bf16[64,2048]{1,0:T(8,128)(2,1)S(1)} %get-tuple-element.60), channel_id=1, source_target_pairs={{0,14},{2,0},{4,2},{6,4},{8,6},{10,8},{12,10},{14,12},{1,15},{3,1}... | collective-permute-start | bytes 786440 | tf_op jit(solution)/shard_map/ppermute | solution.py:18
  203.2 7.7 %collective-permute-start.24 = (bf16[64,2048]{1,0:T(8,128)(2,1)S(1)}, bf16[64,2048]{1,0:T(8,128)(2,1)S(1)}, u32[]{:S(2)}, u32[]{:S(2)}) collective-permute-start(bf16[64,2048]{1,0:T(8,128)(2,1)S(1)} %get-tuple-element.68), channel_id=1, source_target_pairs={{0,2},{2,4},{4,6},{6,8},{8,10},{10,12},{12,14},{14,0},{1,3},{3,5},... | collective-permute-start | bytes 786440 | tf_op jit(solution)/shard_map/ppermute | solution.py:18
  205.3 8.0 %collective-permute-start.26 = (bf16[64,2048]{1,0:T(8,128)(2,1)S(1)}, bf16[64,2048]{1,0:T(8,128)(2,1)S(1)}, u32[]{:S(2)}, u32[]{:S(2)}) collective-permute-start(bf16[64,2048]{1,0:T(8,128)(2,1)S(1)} %get-tuple-element.69), channel_id=1, source_target_pairs={{0,14},{2,0},{4,2},{6,4},{8,6},{10,8},{12,10},{14,12},{1,15},{3,1}... | collective-permute-start | bytes 786440 | tf_op jit(solution)/shard_map/ppermute | solution.py:18
  213.5 7.7 %collective-permute-start.28 = (bf16[64,2048]{1,0:T(8,128)(2,1)S(1)}, bf16[64,2048]{1,0:T(8,128)(2,1)S(1)}, u32[]{:S(2)}, u32[]{:S(2)}) collective-permute-start(bf16[64,2048]{1,0:T(8,128)(2,1)S(1)} %get-tuple-element.67), channel_id=1, source_target_pairs={{0,2},{2,4},{4,6},{6,8},{8,10},{10,12},{12,14},{14,0},{1,3},{3,5},... | collective-permute-start | bytes 786440 | tf_op jit(solution)/shard_map/ppermute | solution.py:18
  213.7 7.5 %collective-permute-start.30 = (bf16[64,2048]{1,0:T(8,128)(2,1)S(1)}, bf16[64,2048]{1,0:T(8,128)(2,1)S(1)}, u32[]{:S(2)}, u32[]{:S(2)}) collective-permute-start(bf16[64,2048]{1,0:T(8,128)(2,1)S(1)} %get-tuple-element.66), channel_id=1, source_target_pairs={{0,14},{2,0},{4,2},{6,4},{8,6},{10,8},{12,10},{14,12},{1,15},{3,1}... | collective-permute-start | bytes 786440 | tf_op jit(solution)/shard_map/ppermute | solution.py:18
